TPU v7x, 512 devices: a whole 4x8x8 slice. The times are simulated.
512 devices in a mesh: inner: 16 (over z_lo, y), blk: 32 (over x, z_hi, core).
Axes of the slice: x: 4, y: 8, z: 8 (z_hi: 4, z_lo: 2; z = z_hi * 2 + z_lo), core: 2. Of those that a mesh axis runs over, the one named last changes fastest.
Arguments:
- image_emb: float32 [12288, 768], P(('inner', 'blk')), may hold values from -150 to 150
- text_emb: float32 [12288, 768], P(('inner', 'blk')), may hold values from -150 to 150
- logit_scale: float32 [1], replicated, may hold values from 30 to 100
Outputs:
- mean_loss: float32 [1], replicated
- image_grad: float32 [12288, 768], P(('inner', 'blk'))
- text_grad: float32 [12288, 768], P(('inner', 'blk'))
All inputs are finite; a program needn't handle non-finite values.
Results may differ from a plain program's by a relative error of at most 0.006.
Values may be sent and summed in bfloat16 or wider, within the bound.
No kernel may reach another device: no remote copies, remote signals or barrier semaphores. Data moves between devices by JAX's collectives and lax.ppermute only.
A program may use at most 64 MiB of HBM per device.

v0:
```python
import jax
import jax.numpy as jnp
from jax import lax
from jax.sharding import Mesh
from jax.sharding import PartitionSpec as P

BLK = ("blk_0", "blk_1", "blk_2")
INNER = ("inner_0", "inner_1")
INNER_BLK = ("inner_0", "inner_1", "blk_0", "blk_1", "blk_2")
EPSILON = 1e-06


def sent_to_all(x, axis):
    copies = jnp.broadcast_to(x, (lax.axis_size(axis), *x.shape))
    return lax.all_to_all(copies, axis, split_axis=0, concat_axis=0, tiled=True)


def in_order(blocks, dim):
    dims = list(blocks.shape[1:])
    dims[dim] *= blocks.shape[0]
    return jnp.moveaxis(blocks, 0, dim).reshape(dims)


def gather_directly(x, axis, dim):
    blocks = sent_to_all(x, axis)
    return in_order(blocks, dim)


def all_in_one(x, axis):
    leaves = jax.tree.leaves(x)
    turns = sorted(range(len(leaves)), key=lambda k: -leaves[k].size)
    width = (1, *leaves[turns[0]].shape)[-1]
    lines = [
        jnp.pad(leaves[k].reshape(-1), (0, -leaves[k].size % width)).reshape(-1, width)
        for k in turns
    ]
    both, at, found = (sent_to_all(jnp.concatenate(lines), axis), 0, {})
    for k, line in zip(turns, lines):
        slab = both[:, at : at + len(line)].reshape(len(both), -1)
        found[k] = slab[:, : leaves[k].size].reshape(-1, *leaves[k].shape)
        at += len(line)
    numbers = iter(range(len(leaves)))
    return jax.tree.map(lambda _: found[next(numbers)], x)


def joined_by_halves(pieces, combine):
    while len(jax.tree.leaves(pieces)[0]) > 1:
        pieces = jax.vmap(combine)(
            *(jax.tree.map(lambda part: part[side::2], pieces) for side in (0, 1))
        )
    return jax.tree.map(lambda part: part[0], pieces)


def combined_all(x, axis, combine):
    pieces = all_in_one(x, axis)
    return joined_by_halves(pieces, combine)


def split_up(x, dim, length):
    before, after = (x.shape[:dim], x.shape[dim + 1 :])
    return jnp.moveaxis(x.reshape(*before, length, -1, *after), dim, 0)


def summed_on_arrival(x, axis, dim):
    length = lax.axis_size(axis)
    blocks = lax.all_to_all(split_up(x, dim, length), axis, 0, 0, tiled=True)
    return jnp.sum(blocks.astype(jnp.float32), axis=0)


def by_axis(x, axes):
    for axis in axes:
        x = lax.psum(x, axis)
    return x


def unit_rows(values):
    inverse = lax.rsqrt(jnp.sum(values * values, axis=1, keepdims=True) + EPSILON)
    return (values * inverse, inverse)


def project(gradient, direction, inverse):
    return (gradient - direction * jnp.sum(gradient * direction, axis=1, keepdims=True)) * inverse


def gather_rows(values, wide_axis):
    if wide_axis:
        return gather_directly(values, BLK, 0)
    return gather_directly(values, INNER, 0)


def combine_stats(former, latter):
    highest = jnp.maximum(former[0], latter[0])
    summed = former[1] * jnp.exp(former[0] - highest) + latter[1] * jnp.exp(latter[0] - highest)
    return (highest, summed)


def merge_stats(peaks, totals, wide_axis):
    if wide_axis:
        peaks, totals = combined_all((peaks, totals), BLK, combine_stats)
    else:
        peaks, totals = combined_all((peaks, totals), INNER, combine_stats)
    return peaks + jnp.log(totals)


def reduce_rows(partial_value, wide_axis):
    if wide_axis:
        return summed_on_arrival(partial_value.astype(jnp.bfloat16), BLK, 0)
    return summed_on_arrival(partial_value.astype(jnp.bfloat16), INNER, 0)


def own_index(wide_axis):
    if wide_axis:
        return lax.axis_index(BLK)
    return lax.axis_index(INNER)


def on_device(image_emb, text_emb, logit_scale):
    own_rows, embed_width = image_emb.shape
    factor = logit_scale[0]
    image_unit, image_inverse = unit_rows(image_emb)
    text_unit, text_inverse = unit_rows(text_emb)
    image_half = image_unit.astype(jnp.bfloat16)
    text_half = text_unit.astype(jnp.bfloat16)
    image_group = gather_rows(image_half, False)
    text_group = gather_rows(text_half, True)
    image_count = image_group.shape[0]
    text_count = text_group.shape[0]
    pieces = max(1, text_count // 128)
    text_blocks = text_group.reshape(pieces, text_count // pieces, embed_width)
    contract_last = (((1,), (1,)), ((), ()))
    contract_first = (((0,), (0,)), ((), ()))

    def scores(text_block):
        return factor * lax.dot_general(
            image_group, text_block, contract_last, preferred_element_type=jnp.float32
        )

    def first_pass(state, text_block):
        row_peak, row_total = state
        logits = scores(text_block)
        new_peak = jnp.maximum(row_peak, jnp.max(logits, axis=1))
        row_total = row_total * jnp.exp(row_peak - new_peak) + jnp.sum(
            jnp.exp(logits - new_peak[:, None]), axis=1
        )
        col_peak = jnp.max(logits, axis=0)
        col_total = jnp.sum(jnp.exp(logits - col_peak[None, :]), axis=0)
        return ((new_peak, row_total), (col_peak, col_total))

    initial = (jnp.full((image_count,), -1e30, jnp.float32), jnp.zeros((image_count,), jnp.float32))
    (row_peak, row_total), (col_peak, col_total) = lax.scan(first_pass, initial, text_blocks)
    row_lse = merge_stats(row_peak, row_total, False)
    col_lse = merge_stats(col_peak.reshape(text_count), col_total.reshape(text_count), True)
    half_factor = 0.5 * factor

    def make_weights(text_block, col_block):
        logits = scores(text_block)
        return (
            half_factor
            * (jnp.exp(logits - row_lse[:, None]) + jnp.exp(logits - col_block[None, :]))
        ).astype(jnp.bfloat16)

    col_blocks = col_lse.reshape(pieces, text_count // pieces)
    empty = jnp.zeros((image_count, embed_width), jnp.float32)

    def second_pass(image_acc, inputs):
        text_block, col_block = inputs
        weights = make_weights(text_block, col_block)
        image_acc = image_acc + jnp.dot(weights, text_block, preferred_element_type=jnp.float32)
        text_part = lax.dot_general(
            weights, image_group, contract_first, preferred_element_type=jnp.float32
        )
        return (image_acc, text_part)

    image_partial, text_parts = lax.scan(second_pass, empty, (text_blocks, col_blocks))
    text_sum = reduce_rows(text_parts.reshape(text_count, embed_width), True)
    image_sum = reduce_rows(image_partial, False)
    diagonal = factor * jnp.sum(
        image_half.astype(jnp.float32) * text_half.astype(jnp.float32), axis=1
    )
    row_own = lax.dynamic_slice_in_dim(row_lse, own_index(False) * own_rows, own_rows)
    col_own = lax.dynamic_slice_in_dim(col_lse, own_index(True) * own_rows, own_rows)
    share = jnp.sum(row_own - diagonal) + jnp.sum(col_own - diagonal)
    whole_count = own_rows * lax.axis_size(INNER) * lax.axis_size(BLK)
    mean_loss = (by_axis(share, INNER_BLK) / (2.0 * whole_count)).reshape(1)
    image_pull = image_sum - factor * text_half.astype(jnp.float32)
    text_pull = text_sum - factor * image_half.astype(jnp.float32)
    image_grad = project(image_pull, image_unit, image_inverse)
    text_grad = project(text_pull, text_unit, text_inverse)
    return (mean_loss, image_grad, text_grad)


def solution(mesh):
    split = Mesh(
        mesh.devices.reshape(2, 8, 4, 4, 2), ("inner_0", "inner_1", "blk_0", "blk_1", "blk_2")
    )
    in_specs = (P(INNER_BLK, None), P(INNER_BLK, None), P())
    out_specs = (P(), P(INNER_BLK, None), P(INNER_BLK, None))
    return jax.shard_map(
        on_device, mesh=split, in_specs=in_specs, out_specs=out_specs, check_vma=False
    )
```

profile of v0, /device:TPU:1, one launch (start us, length us, event | category | flops | bytes accessed | tf_op | source)
XLA Modules:
  0.0 240.1 jit_solution(7228179052295470135)
XLA Ops:
  0.6 1.0 multiply_reduce_fusion.2
  1.7 1.0 multiply_convert_fusion.1
  2.6 0.8 broadcast_in_dim.46
  3.5 9.6 %all-to-all-start.1 = ((bf16[16,24,768]{2,1,0:T(8,128)(2,1)}), bf16[16,24,768]{2,1,0:T(8,128)(2,1)S(1)}, u32[]{:S(2)}, u32[]{:S(2)}) async-start(bf16[16,24,768]{2,1,0:T(8,128)(2,1)} %broadcast_in_dim.46), calls=%async_computation.1 | async-start | bytes 1179648 | tf_op jit(solution)/shard_map/all_to_all | solution.py:15
  13.3 14.8 %all-to-all-done.1 = bf16[16,24,768]{2,1,0:T(8,128)(2,1)S(1)} async-done(((bf16[16,24,768]{2,1,0:T(8,128)(2,1)}), bf16[16,24,768]{2,1,0:T(8,128)(2,1)S(1)}, u32[]{:S(2)}, u32[]{:S(2)}) %all-to-all-start.1) | async-done | bytes 589856 | tf_op jit(solution)/shard_map/all_to_all | solution.py:15
  28.1 1.1 broadcast_in_dim.45
  29.3 14.8 %all-to-all-start = ((bf16[32,24,768]{2,1,0:T(8,128)(2,1)}), bf16[32,24,768]{2,1,0:T(8,128)(2,1)S(1)}, u32[]{:S(2)}, u32[]{:S(2)}) async-start(bf16[32,24,768]{2,1,0:T(8,128)(2,1)} %broadcast_in_dim.45), calls=%async_computation | async-start | bytes 2359296 | tf_op jit(solution)/shard_map/all_to_all | solution.py:15
  44.8 30.6 %all-to-all-done = bf16[32,24,768]{2,1,0:T(8,128)(2,1)S(1)} async-done(((bf16[32,24,768]{2,1,0:T(8,128)(2,1)}), bf16[32,24,768]{2,1,0:T(8,128)(2,1)S(1)}, u32[]{:S(2)}, u32[]{:S(2)}) %all-to-all-start) | async-done | bytes 1179680 | tf_op jit(solution)/shard_map/all_to_all | solution.py:15
  75.3 8.2 %while.30 = (s32[]{:T(128)}, f32[384]{0:T(512)S(1)}, f32[384]{0:T(512)S(1)}, f32[6,128]{1,0:T(8,128)S(1)}, f32[6,128]{1,0:T(8,128)S(1)}, /*index=5*/f32[]{:T(128...) while((s32[]{:T(128)}, f32[384]{0:T(512)S(1)}, ...), condition=%wide.region_7.8_spmd.clone, body=%wide.region_2.7_spmd.clone.sunk | while | flops 75843200 | bytes 1203328 | solution.py:150
  75.3 1.1 fusion.45
  76.7 1.1 fusion.45
  78.1 1.1 fusion.45
  79.5 1.1 fusion.45
  80.8 1.1 fusion.45
  82.2 1.1 fusion.45
  83.6 0.6 broadcast_in_dim.47
  84.3 5.6 %all-to-all-start.2 = ((f32[16,2,384]{2,1,0:T(2,128)}), f32[16,2,384]{2,1,0:T(2,128)S(1)}, u32[]{:S(2)}, u32[]{:S(2)}) async-start(f32[16,2,384]{2,1,0:T(2,128)} %broadcast_in_dim.47), calls=%async_computation.2 | async-start | bytes 98304 | tf_op jit(solution)/shard_map/all_to_all | solution.py:15
  89.9 7.3 %all-to-all-done.2 = f32[16,2,384]{2,1,0:T(2,128)S(1)} async-done(((f32[16,2,384]{2,1,0:T(2,128)}), f32[16,2,384]{2,1,0:T(2,128)S(1)}, u32[]{:S(2)}, u32[]{:S(2)}) %all-to-all-start.2) | async-done | bytes 49184 | tf_op jit(solution)/shard_map/all_to_all | solution.py:15
  97.2 0.7 broadcast_in_dim.48
  98.0 6.0 %all-to-all-start.3 = ((f32[32,2,768]{2,1,0:T(2,128)}), f32[32,2,768]{2,1,0:T(2,128)S(1)}, u32[]{:S(2)}, u32[]{:S(2)}) async-start(f32[32,2,768]{2,1,0:T(2,128)} %broadcast_in_dim.48), calls=%async_computation.3 | async-start | bytes 393216 | tf_op jit(solution)/shard_map/all_to_all | solution.py:15
  104.4 11.3 %all-to-all-done.3 = f32[32,2,768]{2,1,0:T(2,128)S(1)} async-done(((f32[32,2,768]{2,1,0:T(2,128)}), f32[32,2,768]{2,1,0:T(2,128)S(1)}, u32[]{:S(2)}, u32[]{:S(2)}) %all-to-all-start.3) | async-done | bytes 196640 | tf_op jit(solution)/shard_map/all_to_all | solution.py:15
  116.5 14.9 %while.31 = (s32[]{:T(128)}, f32[384,768]{1,0:T(8,128)S(1)}, bf16[6,128,768]{2,1,0:T(8,128)(2,1)}, f32[]{:T(128)}, f32[]{:T(128)}, /*index=5*/bf16[6,128,768]{2,...) while((s32[]{:T(128)}, f32[384,768]{1,0:T(8,128)S(1)}, ...), condition=%wide.region_17.18_spmd.clone, body=%wide.region_16.17_spmd.clone.sunk | while | flops 227377152 | bytes 4624523 | solution.py:174
  116.5 1.0 multiply_convert_fusion.4
  117.5 0.5 convolution_add_fusion.2
  118.0 0.9 fusion.54
  119.0 1.0 multiply_convert_fusion.4
  120.0 0.5 convolution_add_fusion.2
  120.5 0.9 fusion.54
  121.5 1.0 multiply_convert_fusion.4
  122.5 0.5 convolution_add_fusion.2
  123.0 0.9 fusion.54
  123.9 1.0 multiply_convert_fusion.4
  124.9 0.5 convolution_add_fusion.2
  125.5 0.9 fusion.54
  126.4 1.0 multiply_convert_fusion.4
  127.9 0.9 fusion.54
  128.9 1.0 multiply_convert_fusion.4
  130.4 0.9 fusion.54
  131.4 20.4 %all_to_all.30 = bf16[16,24,768]{2,1,0:T(8,128)(2,1)S(1)} all-to-all(bf16[16,24,768]{2,1,0:T(8,128)(2,1)S(1)} %bitcast.92), channel_id=1, replica_groups=mesh['inner_0'=2,'inner_1'=8,'blk_0'=4,'blk_1'=4,'blk_2'=2] {'inner_0','..., dimensions={0} | all-to-all | bytes 1179648 | tf_op jit(solution)/shard_map/all_to_all | solution.py:66
  151.8 5.9 %all-to-all-start.5 = ((bf16[32,24,768]{2,1,0:T(8,128)(2,1)}), bf16[32,24,768]{2,1,0:T(8,128)(2,1)S(1)}, u32[]{:S(2)}, u32[]{:S(2)}) async-start(bf16[32,24,768]{2,1,0:T(8,128)(2,1)} %bitcast.9), calls=%async_computation.5 | async-start | bytes 2359296 | tf_op jit(solution)/shard_map/all_to_all | solution.py:66
  157.9 31.1 %all-to-all-done.5 = bf16[32,24,768]{2,1,0:T(8,128)(2,1)S(1)} async-done(((bf16[32,24,768]{2,1,0:T(8,128)(2,1)}), bf16[32,24,768]{2,1,0:T(8,128)(2,1)S(1)}, u32[]{:S(2)}, u32[]{:S(2)}) %all-to-all-start.5) | async-done | bytes 1179680 | tf_op jit(solution)/shard_map/all_to_all | solution.py:66
  189.4 0.7 fusion.21
  191.4 4.3 %psum.35 = f32[]{:T(128)} all-reduce(f32[]{:T(128)S(6)} %add.121), channel_id=1, replica_groups=mesh['inner_0'=2,'inner_1'=8,'blk_0'=4,'blk_1'=4,'blk_2'=2] {'inner_0'}, use_global_device_ids=true, to_apply=%region_11.12 | all-reduce | flops 1 | bytes 8 | tf_op jit(solution)/shard_map/psum | solution.py:72
  195.7 12.1 %psum.36 = f32[]{:T(128)} all-reduce(f32[]{:T(128)} %psum.35), channel_id=1, replica_groups=mesh['inner_0'=2,'inner_1'=8,'blk_0'=4,'blk_1'=4,'blk_2'=2] {'inner_1'}, use_global_device_ids=true, to_apply=%region_12.13 | all-reduce | flops 1 | bytes 8 | tf_op jit(solution)/shard_map/psum | solution.py:72
  207.8 7.9 %psum.37 = f32[]{:T(128)} all-reduce(f32[]{:T(128)} %psum.36), channel_id=1, replica_groups=mesh['inner_0'=2,'inner_1'=8,'blk_0'=4,'blk_1'=4,'blk_2'=2] {'blk_0'}, use_global_device_ids=true, to_apply=%region_13.14 | all-reduce | flops 1 | bytes 8 | tf_op jit(solution)/shard_map/psum | solution.py:72
  215.7 9.7 %psum.38 = f32[]{:T(128)} all-reduce(f32[]{:T(128)} %psum.37), channel_id=1, replica_groups=mesh['inner_0'=2,'inner_1'=8,'blk_0'=4,'blk_1'=4,'blk_2'=2] {'blk_1'}, use_global_device_ids=true, to_apply=%region_14.15 | all-reduce | flops 1 | bytes 8 | tf_op jit(solution)/shard_map/psum | solution.py:72
  225.4 12.2 %psum.39 = f32[]{:T(128)} all-reduce(f32[]{:T(128)} %psum.38), channel_id=1, replica_groups=mesh['inner_0'=2,'inner_1'=8,'blk_0'=4,'blk_1'=4,'blk_2'=2] {'blk_2'}, use_global_device_ids=true, to_apply=%region_15.16 | all-reduce | flops 1 | bytes 8 | tf_op jit(solution)/shard_map/psum | solution.py:72
  238.2 0.8 subtract_multiply_fusion
  (111 shorter events, 4.6 us)
Async XLA Ops:
  0.6 12.4 %copy-start = (f32[24,768]{1,0:T(8,128)S(1)}, f32[24,768]{1,0:T(8,128)}, u32[]{:S(2)}) copy-start(f32[24,768]{1,0:T(8,128)} %param.8) | copy-start | bytes 221188
  3.5 24.6 %all-to-all-start.1 = ((bf16[16,24,768]{2,1,0:T(8,128)(2,1)}), bf16[16,24,768]{2,1,0:T(8,128)(2,1)S(1)}, u32[]{:S(2)}, u32[]{:S(2)}) async-start(bf16[16,24,768]{2,1,0:T(8,128)(2,1)} %broadcast_in_dim.46), calls=%async_computation.1 | async-start | bytes 1179648 | tf_op jit(solution)/shard_map/all_to_all | solution.py:15
  29.3 46.1 %all-to-all-start = ((bf16[32,24,768]{2,1,0:T(8,128)(2,1)}), bf16[32,24,768]{2,1,0:T(8,128)(2,1)S(1)}, u32[]{:S(2)}, u32[]{:S(2)}) async-start(bf16[32,24,768]{2,1,0:T(8,128)(2,1)} %broadcast_in_dim.45), calls=%async_computation | async-start | bytes 2359296 | tf_op jit(solution)/shard_map/all_to_all | solution.py:15
  84.3 13.0 %all-to-all-start.2 = ((f32[16,2,384]{2,1,0:T(2,128)}), f32[16,2,384]{2,1,0:T(2,128)S(1)}, u32[]{:S(2)}, u32[]{:S(2)}) async-start(f32[16,2,384]{2,1,0:T(2,128)} %broadcast_in_dim.47), calls=%async_computation.2 | async-start | bytes 98304 | tf_op jit(solution)/shard_map/all_to_all | solution.py:15
  98.0 17.8 %all-to-all-start.3 = ((f32[32,2,768]{2,1,0:T(2,128)}), f32[32,2,768]{2,1,0:T(2,128)S(1)}, u32[]{:S(2)}, u32[]{:S(2)}) async-start(f32[32,2,768]{2,1,0:T(2,128)} %broadcast_in_dim.48), calls=%async_computation.3 | async-start | bytes 393216 | tf_op jit(solution)/shard_map/all_to_all | solution.py:15
  151.8 37.2 %all-to-all-start.5 = ((bf16[32,24,768]{2,1,0:T(8,128)(2,1)}), bf16[32,24,768]{2,1,0:T(8,128)(2,1)S(1)}, u32[]{:S(2)}, u32[]{:S(2)}) async-start(bf16[32,24,768]{2,1,0:T(8,128)(2,1)} %bitcast.9), calls=%async_computation.5 | async-start | bytes 2359296 | tf_op jit(solution)/shard_map/all_to_all | solution.py:66
  157.7 31.4 %copy-start.1 = (f32[24,768]{1,0:T(8,128)S(1)}, f32[24,768]{1,0:T(8,128)}, u32[]{:S(2)}) copy-start(f32[24,768]{1,0:T(8,128)} %param.7) | copy-start | bytes 221188
where the time goes:
time: 241 us; the launch traced here: 240 us
  waiting for transfers between devices  95.2 us (40%)
  blocking collectives  66.6 us (28%)
  starting transfers between devices  41.9 us (17%)
  matrix products  21 us (9%)
  other arithmetic  5.69 us (2%)
  between operations  4.68 us (2%)
  local copies, waits for them, and re-layouts  4.64 us (2%)
    all_to_all x4, waiting for transfers between devices, sent_to_all(): return lax.all_to_all(copies, axis, split_axis=0, concat_axis=0, tiled=True)  64.1 us
    psum x5, blocking collectives, by_axis(): x = lax.psum(x, axis)  46.2 us
    all_to_all x4, starting transfers between devices, sent_to_all(): return lax.all_to_all(copies, axis, split_axis=0, concat_axis=0, tiled=True)  36 us
    all_to_all x1, waiting for transfers between devices, summed_on_arrival(): blocks = lax.all_to_all(split_up(x, dim, length), axis, 0, 0, tiled=True)  31.1 us
    all_to_all x1, blocking collectives, summed_on_arrival(): blocks = lax.all_to_all(split_up(x, dim, length), axis, 0, 0, tiled=True)  20.4 us
    dot_general x12, matrix products, scores(): lax.dot_general(image_group, text_block, contract_last, preferred_element...  12.3 us
    all_to_all x1, starting transfers between devices, summed_on_arrival(): blocks = lax.all_to_all(split_up(x, dim, length), axis, 0, 0, tiled=True)  5.93 us
    dot_general x6, matrix products, second_pass(): lax.dot_general(weights, image_group, contract_first, preferred_element_t...  5.64 us
  transfers between devices with their start and end apart: 5, of which 5 were waited for; matrix products, arithmetic and copies ran while one was open for 0% of the time, Pallas kernels for 0%

commit v1 on v0

--- a/solution.py
+++ b/solution.py
@@ -69,7 +69,7 @@
 
 def by_axis(x, axes):
     for axis in axes:
-        x = lax.psum(x, axis)
+        x = jnp.sum(lax.all_gather(x, axis), axis=0)
     return x
 
 

time: 241 us -> 253 us (1.050)
  local copies, waits for them, and re-layouts: 4.64 us -> 17.4 us
  blocking collectives: 66.6 us -> 63.5 us
  other arithmetic: 5.69 us -> 8.7 us
    psum x5 -> x0, blocking collectives: 46.2 us -> none  [by_axis(): x = lax.psum(x, axis)]
    unnamed x0 -> x5, blocking collectives: none -> 43.1 us
    unnamed x10 -> x25, local copies, waits for them, and re-layouts: 0.04 us -> 12.8 us
    reduce_sum x0 -> x5, other arithmetic: none -> 3.02 us  [by_axis(): x = jnp.sum(lax.all_gather(x, axis), axis=0)]
  transfers between devices with their start and end apart: 5 -> 5, of which waited for: 5 -> 5; matrix products, arithmetic and copies ran while one was open for 0% -> 1% of each run, Pallas kernels for 0% -> 0%
where the time goes in v1:
time: 253 us; the launch traced here: 251 us
  waiting for transfers between devices  93.9 us (37%)
  blocking collectives  63.5 us (25%)
  starting transfers between devices  41.9 us (17%)
  matrix products  21 us (8%)
  local copies, waits for them, and re-layouts  17.4 us (7%)
  other arithmetic  8.7 us (3%)
  between operations  4.69 us (2%)
    all_to_all x4, waiting for transfers between devices, sent_to_all(): return lax.all_to_all(copies, axis, split_axis=0, concat_axis=0, tiled=True)  64.1 us
    unnamed x5, blocking collectives  43.1 us
    all_to_all x4, starting transfers between devices, sent_to_all(): return lax.all_to_all(copies, axis, split_axis=0, concat_axis=0, tiled=True)  36 us
    all_to_all x1, waiting for transfers between devices, summed_on_arrival(): blocks = lax.all_to_all(split_up(x, dim, length), axis, 0, 0, tiled=True)  29.8 us
    all_to_all x1, blocking collectives, summed_on_arrival(): blocks = lax.all_to_all(split_up(x, dim, length), axis, 0, 0, tiled=True)  20.4 us
    unnamed x25, local copies, waits for them, and re-layouts  12.8 us
    dot_general x12, matrix products, scores(): lax.dot_general(image_group, text_block, contract_last, preferred_element...  12.3 us
    all_to_all x1, starting transfers between devices, summed_on_arrival(): blocks = lax.all_to_all(split_up(x, dim, length), axis, 0, 0, tiled=True)  5.93 us
  transfers between devices with their start and end apart: 5, of which 5 were waited for; matrix products, arithmetic and copies ran while one was open for 1% of the time, Pallas kernels for 0%

profile of v1, /device:TPU:1, one launch (start us, length us, event | category | flops | bytes accessed | tf_op | source)
XLA Modules:
  0.0 251.5 jit_solution(1161529222767986425)
XLA Ops:
  0.6 1.0 multiply_reduce_fusion.2
  1.7 1.0 multiply_convert_fusion.1
  3.5 9.6 %all-to-all-start.1 = ((bf16[16,24,768]{2,1,0:T(8,128)(2,1)}), bf16[16,24,768]{2,1,0:T(8,128)(2,1)S(1)}, u32[]{:S(2)}, u32[]{:S(2)}) async-start(bf16[16,24,768]{2,1,0:T(8,128)(2,1)} %broadcast_in_dim.46), calls=%async_computation.1 | async-start | bytes 1179648 | tf_op jit(solution)/shard_map/all_to_all | solution.py:15
  13.3 14.8 %all-to-all-done.1 = bf16[16,24,768]{2,1,0:T(8,128)(2,1)S(1)} async-done(((bf16[16,24,768]{2,1,0:T(8,128)(2,1)}), bf16[16,24,768]{2,1,0:T(8,128)(2,1)S(1)}, u32[]{:S(2)}, u32[]{:S(2)}) %all-to-all-start.1) | async-done | bytes 589856 | tf_op jit(solution)/shard_map/all_to_all | solution.py:15
  28.1 1.1 broadcast_in_dim.45
  29.3 14.8 %all-to-all-start = ((bf16[32,24,768]{2,1,0:T(8,128)(2,1)}), bf16[32,24,768]{2,1,0:T(8,128)(2,1)S(1)}, u32[]{:S(2)}, u32[]{:S(2)}) async-start(bf16[32,24,768]{2,1,0:T(8,128)(2,1)} %broadcast_in_dim.45), calls=%async_computation | async-start | bytes 2359296 | tf_op jit(solution)/shard_map/all_to_all | solution.py:15
  44.8 30.6 %all-to-all-done = bf16[32,24,768]{2,1,0:T(8,128)(2,1)S(1)} async-done(((bf16[32,24,768]{2,1,0:T(8,128)(2,1)}), bf16[32,24,768]{2,1,0:T(8,128)(2,1)S(1)}, u32[]{:S(2)}, u32[]{:S(2)}) %all-to-all-start) | async-done | bytes 1179680 | tf_op jit(solution)/shard_map/all_to_all | solution.py:15
  75.3 8.2 %while.30 = (s32[]{:T(128)}, f32[384]{0:T(512)S(1)}, f32[384]{0:T(512)S(1)}, f32[6,128]{1,0:T(8,128)S(1)}, f32[6,128]{1,0:T(8,128)S(1)}, /*index=5*/f32[]{:T(128...) while((s32[]{:T(128)}, f32[384]{0:T(512)S(1)}, ...), condition=%wide.region_7.8_spmd.clone, body=%wide.region_2.7_spmd.clone.sunk | while | flops 75843200 | bytes 1203328 | solution.py:150
  75.3 1.1 fusion.45
  76.7 1.1 fusion.45
  78.1 1.1 fusion.45
  79.5 1.1 fusion.45
  80.8 1.1 fusion.45
  82.2 1.1 fusion.45
  84.3 5.6 %all-to-all-start.2 = ((f32[16,2,384]{2,1,0:T(2,128)}), f32[16,2,384]{2,1,0:T(2,128)S(1)}, u32[]{:S(2)}, u32[]{:S(2)}) async-start(f32[16,2,384]{2,1,0:T(2,128)} %broadcast_in_dim.47), calls=%async_computation.2 | async-start | bytes 98304 | tf_op jit(solution)/shard_map/all_to_all | solution.py:15
  89.9 7.3 %all-to-all-done.2 = f32[16,2,384]{2,1,0:T(2,128)S(1)} async-done(((f32[16,2,384]{2,1,0:T(2,128)}), f32[16,2,384]{2,1,0:T(2,128)S(1)}, u32[]{:S(2)}, u32[]{:S(2)}) %all-to-all-start.2) | async-done | bytes 49184 | tf_op jit(solution)/shard_map/all_to_all | solution.py:15
  98.0 6.0 %all-to-all-start.3 = ((f32[32,2,768]{2,1,0:T(2,128)}), f32[32,2,768]{2,1,0:T(2,128)S(1)}, u32[]{:S(2)}, u32[]{:S(2)}) async-start(f32[32,2,768]{2,1,0:T(2,128)} %broadcast_in_dim.48), calls=%async_computation.3 | async-start | bytes 393216 | tf_op jit(solution)/shard_map/all_to_all | solution.py:15
  104.4 11.3 %all-to-all-done.3 = f32[32,2,768]{2,1,0:T(2,128)S(1)} async-done(((f32[32,2,768]{2,1,0:T(2,128)}), f32[32,2,768]{2,1,0:T(2,128)S(1)}, u32[]{:S(2)}, u32[]{:S(2)}) %all-to-all-start.3) | async-done | bytes 196640 | tf_op jit(solution)/shard_map/all_to_all | solution.py:15
  116.5 14.9 %while.31 = (s32[]{:T(128)}, f32[384,768]{1,0:T(8,128)S(1)}, bf16[6,128,768]{2,1,0:T(8,128)(2,1)}, f32[]{:T(128)}, f32[]{:T(128)}, /*index=5*/bf16[6,128,768]{2,...) while((s32[]{:T(128)}, f32[384,768]{1,0:T(8,128)S(1)}, ...), condition=%wide.region_17.18_spmd.clone, body=%wide.region_16.17_spmd.clone.sunk | while | flops 227377152 | bytes 4624523 | solution.py:174
  116.5 1.0 multiply_convert_fusion.4
  118.0 0.9 fusion.54
  119.0 1.0 multiply_convert_fusion.4
  120.5 0.9 fusion.54
  121.5 1.0 multiply_convert_fusion.4
  123.0 0.9 fusion.54
  123.9 1.0 multiply_convert_fusion.4
  125.5 0.9 fusion.54
  126.4 1.0 multiply_convert_fusion.4
  127.9 0.9 fusion.54
  128.9 1.0 multiply_convert_fusion.4
  130.4 0.9 fusion.54
  131.4 20.4 %all_to_all.30 = bf16[16,24,768]{2,1,0:T(8,128)(2,1)S(1)} all-to-all(bf16[16,24,768]{2,1,0:T(8,128)(2,1)S(1)} %bitcast.102), channel_id=1, replica_groups=mesh['inner_0'=2,'inner_1'=8,'blk_0'=4,'blk_1'=4,'blk_2'=2] {'inner_0','..., dimensions={0} | all-to-all | bytes 1179648 | tf_op jit(solution)/shard_map/all_to_all | solution.py:66
  151.8 5.9 %all-to-all-start.5 = ((bf16[32,24,768]{2,1,0:T(8,128)(2,1)}), bf16[32,24,768]{2,1,0:T(8,128)(2,1)S(1)}, u32[]{:S(2)}, u32[]{:S(2)}) async-start(bf16[32,24,768]{2,1,0:T(8,128)(2,1)} %bitcast.19), calls=%async_computation.5 | async-start | bytes 2359296 | tf_op jit(solution)/shard_map/all_to_all | solution.py:66
  157.8 1.3 dynamic-slice.2
  159.2 29.8 %all-to-all-done.5 = bf16[32,24,768]{2,1,0:T(8,128)(2,1)S(1)} async-done(((bf16[32,24,768]{2,1,0:T(8,128)(2,1)}), bf16[32,24,768]{2,1,0:T(8,128)(2,1)S(1)}, u32[]{:S(2)}, u32[]{:S(2)}) %all-to-all-start.5) | async-done | bytes 1179680 | tf_op jit(solution)/shard_map/all_to_all | solution.py:66
  192.1 1.3 dynamic-slice.3
  193.4 3.8 %all-reduce = f32[2]{0:T(128)S(1)} all-reduce(f32[2]{0:T(128)S(1)} %dynamic-update-slice), channel_id=1, replica_groups=mesh['inner_0'=2,'inner_1'=8,'blk_0'=4,'blk_1'=4,'blk_2'=2] {'inner_0'}, use_global_device_ids=true, to_apply=%add | all-reduce | flops 2 | bytes 16
  197.8 1.4 dynamic-update-slice.1
  199.2 1.3 dynamic-slice.4
  200.4 11.5 %all-reduce.1 = f32[8]{0:T(128)S(1)} all-reduce(f32[8]{0:T(128)S(1)} %dynamic-update-slice.1), channel_id=1, replica_groups=mesh['inner_0'=2,'inner_1'=8,'blk_0'=4,'blk_1'=4,'blk_2'=2] {'inner_1'}, use_global_device_ids=true, to_apply=%add.1 | all-reduce | flops 8 | bytes 64
  212.5 1.4 dynamic-update-slice.2
  213.9 1.3 dynamic-slice.5
  215.2 7.2 %all-reduce.2 = f32[4]{0:T(128)S(1)} all-reduce(f32[4]{0:T(128)S(1)} %dynamic-update-slice.2), channel_id=1, replica_groups=mesh['inner_0'=2,'inner_1'=8,'blk_0'=4,'blk_1'=4,'blk_2'=2] {'blk_0'}, use_global_device_ids=true, to_apply=%add.2 | all-reduce | flops 4 | bytes 32
  223.0 1.4 dynamic-update-slice.3
  224.4 1.3 dynamic-slice.6
  225.7 8.8 %all-reduce.3 = f32[4]{0:T(128)S(1)} all-reduce(f32[4]{0:T(128)S(1)} %dynamic-update-slice.3), channel_id=1, replica_groups=mesh['inner_0'=2,'inner_1'=8,'blk_0'=4,'blk_1'=4,'blk_2'=2] {'blk_1'}, use_global_device_ids=true, to_apply=%add.3 | all-reduce | flops 4 | bytes 32
  235.1 1.4 dynamic-update-slice.4
  236.5 11.8 %all-reduce.4 = f32[2]{0:T(128)S(1)} all-reduce(f32[2]{0:T(128)S(1)} %dynamic-update-slice.4), channel_id=1, replica_groups=mesh['inner_0'=2,'inner_1'=8,'blk_0'=4,'blk_1'=4,'blk_2'=2] {'blk_2'}, use_global_device_ids=true, to_apply=%add.4 | all-reduce | flops 2 | bytes 16
  (131 shorter events, 14.1 us)
Async XLA Ops:
  0.6 12.4 %copy-start = (f32[24,768]{1,0:T(8,128)S(1)}, f32[24,768]{1,0:T(8,128)}, u32[]{:S(2)}) copy-start(f32[24,768]{1,0:T(8,128)} %param.8) | copy-start | bytes 221188
  3.5 24.6 %all-to-all-start.1 = ((bf16[16,24,768]{2,1,0:T(8,128)(2,1)}), bf16[16,24,768]{2,1,0:T(8,128)(2,1)S(1)}, u32[]{:S(2)}, u32[]{:S(2)}) async-start(bf16[16,24,768]{2,1,0:T(8,128)(2,1)} %broadcast_in_dim.46), calls=%async_computation.1 | async-start | bytes 1179648 | tf_op jit(solution)/shard_map/all_to_all | solution.py:15
  29.3 46.1 %all-to-all-start = ((bf16[32,24,768]{2,1,0:T(8,128)(2,1)}), bf16[32,24,768]{2,1,0:T(8,128)(2,1)S(1)}, u32[]{:S(2)}, u32[]{:S(2)}) async-start(bf16[32,24,768]{2,1,0:T(8,128)(2,1)} %broadcast_in_dim.45), calls=%async_computation | async-start | bytes 2359296 | tf_op jit(solution)/shard_map/all_to_all | solution.py:15
  84.3 13.0 %all-to-all-start.2 = ((f32[16,2,384]{2,1,0:T(2,128)}), f32[16,2,384]{2,1,0:T(2,128)S(1)}, u32[]{:S(2)}, u32[]{:S(2)}) async-start(f32[16,2,384]{2,1,0:T(2,128)} %broadcast_in_dim.47), calls=%async_computation.2 | async-start | bytes 98304 | tf_op jit(solution)/shard_map/all_to_all | solution.py:15
  98.0 17.8 %all-to-all-start.3 = ((f32[32,2,768]{2,1,0:T(2,128)}), f32[32,2,768]{2,1,0:T(2,128)S(1)}, u32[]{:S(2)}, u32[]{:S(2)}) async-start(f32[32,2,768]{2,1,0:T(2,128)} %broadcast_in_dim.48), calls=%async_computation.3 | async-start | bytes 393216 | tf_op jit(solution)/shard_map/all_to_all | solution.py:15
  151.8 37.2 %all-to-all-start.5 = ((bf16[32,24,768]{2,1,0:T(8,128)(2,1)}), bf16[32,24,768]{2,1,0:T(8,128)(2,1)S(1)}, u32[]{:S(2)}, u32[]{:S(2)}) async-start(bf16[32,24,768]{2,1,0:T(8,128)(2,1)} %bitcast.19), calls=%async_computation.5 | async-start | bytes 2359296 | tf_op jit(solution)/shard_map/all_to_all | solution.py:66
  157.7 31.4 %copy-start.1 = (f32[24,768]{1,0:T(8,128)S(1)}, f32[24,768]{1,0:T(8,128)}, u32[]{:S(2)}) copy-start(f32[24,768]{1,0:T(8,128)} %param.7) | copy-start | bytes 221188
